TPU v7x, 32 devices: a whole 2x2x4 slice. The times are simulated.
32 devices in a mesh: macro: 4 (over y, core), pool: 8 (over z, x).
Axes of the slice: x: 2, y: 2, z: 4, core: 2. Of those that a mesh axis runs over, the one named last changes fastest.
Arguments:
- panels: bfloat16 [8, 768, 768], P('pool', 'macro'), as said below
- loads: float32 [8, 9, 768], P('pool'), may hold values from -6 to 6
- family: int32 [2048, 1], P(('macro', 'pool')), may hold values from 0 to 7; in each aligned block of 64 rows (0 to 63, 64 to 127, ...) at most 8 rows name the same one
- contact: float32 [2048, 768], P(('macro', 'pool')), may hold values from 0.05 to 8
- strain: float32 [2048, 9], P(('macro', 'pool')), may hold values from -6 to 6
- previous: bfloat16 [2048, 6912], P(('macro', 'pool')), may hold values from -3 to 3
Outputs:
- fluct: bfloat16 [2048, 6912], P(('macro', 'pool'))
- stress: float32 [2048, 9], P(('macro', 'pool'))
- tangent: float32 [2048, 81], P(('macro', 'pool'))
Inputs may be any that keep to these rules, and one draw needn't show every extreme that they name: Within the rows of one device no family is named more than 8 times, a bound that some block reaches. `panels`: each panel is symmetric and positive definite.
All inputs are finite; a program needn't handle non-finite values.
Results may differ from a plain program's by a relative error of at most 0.0085.
Values may be sent and summed in bfloat16 or wider, within the bound.
A program may use at most 64 MiB of HBM per device.

v0:
```python
import jax
import jax.numpy as jnp
from jax import lax
from jax.sharding import PartitionSpec as P

DOF = 768
RHS = 9
ITERS = 4
CAP = 8


def for_sending(shard):

    def short(part):
        return part.astype(jnp.bfloat16) if part.dtype == jnp.float32 else part

    return jax.tree.map(short, shard)


def solve_cells(panel, load, contact_rows, previous_rows, strain_rows):
    cells = contact_rows.shape[0]
    width = panel.shape[0]
    count = load.shape[0]
    stiff = panel.astype(jnp.float32)
    inverse = 1.0 / jnp.diagonal(stiff)

    def apply_stiffness(field):
        flat = field.reshape(cells * count, width)
        product = jnp.dot(flat, stiff, precision=lax.Precision.HIGHEST).reshape(cells, count, width)
        return product + contact_rows[:, None, :] * field

    iterate = previous_rows.astype(jnp.float32).reshape(cells, count, width)
    residual = load[None, :, :] - apply_stiffness(iterate)
    scaled = inverse * residual
    direction = scaled
    current = jnp.sum(residual * scaled, axis=-1)
    for sweep in range(ITERS):
        image = apply_stiffness(direction)
        step_size = current / (jnp.sum(direction * image, axis=-1) + 1e-06)
        iterate = iterate + step_size[:, :, None] * direction
        residual = residual - step_size[:, :, None] * image
        scaled = inverse * residual
        updated = jnp.sum(residual * scaled, axis=-1)
        direction = scaled + (updated / (current + 1e-06))[:, :, None] * direction
        current = updated
    tangent = jnp.einsum("sik,jk->sij", iterate, load, precision=lax.Precision.HIGHEST) / width
    stress = jnp.einsum("sij,sj->si", tangent, strain_rows, precision=lax.Precision.HIGHEST)
    return (
        iterate.astype(jnp.bfloat16).reshape(cells, count * width),
        stress,
        tangent.reshape(cells, count * count),
    )


def pick_rows(picking, previous, contact, strain):
    chosen_previous = jnp.dot(
        picking.astype(jnp.bfloat16), previous, preferred_element_type=jnp.float32
    ).astype(jnp.bfloat16)
    weights = picking.astype(jnp.float32)
    chosen_contact = jnp.dot(weights, contact, precision=lax.Precision.HIGHEST)
    chosen_strain = jnp.dot(weights, strain, precision=lax.Precision.HIGHEST)
    return (chosen_previous, chosen_contact, chosen_strain)


def on_device(panels, loads, family, contact, strain, previous):
    full = lax.all_gather(panels, "macro", axis=1, tiled=True)
    groups = lax.axis_size("pool")
    family_ids = family[:, 0]
    one_hot = (family_ids[:, None] == jnp.arange(groups, dtype=jnp.int32)[None, :]).astype(
        jnp.int32
    )
    rank_in = jnp.sum(jnp.cumsum(one_hot, axis=0) * one_hot, axis=1) - 1
    slot_ids = family_ids * CAP + rank_in
    placing = slot_ids[None, :] == jnp.arange(groups * CAP, dtype=jnp.int32)[:, None]
    chosen_previous, chosen_contact, chosen_strain = pick_rows(placing, previous, contact, strain)
    send_previous = chosen_previous.reshape(groups, CAP, RHS * DOF)
    send_contact = chosen_contact.reshape(groups, CAP, DOF)
    send_strain = chosen_strain.reshape(groups, CAP, RHS)
    previous_in = lax.all_to_all(send_previous, "pool", split_axis=0, concat_axis=0, tiled=True)
    contact_in = lax.all_to_all(
        send_contact.astype(jnp.bfloat16), "pool", split_axis=0, concat_axis=0, tiled=True
    ).astype(send_contact.dtype)
    strain_in = lax.all_to_all(
        send_strain.astype(jnp.bfloat16), "pool", split_axis=0, concat_axis=0, tiled=True
    ).astype(send_strain.dtype)
    senders = previous_in.shape[0]
    count = previous_in.shape[1]
    new_rows, stress_rows, tangent_rows = solve_cells(
        full[0],
        loads[0],
        contact_in.reshape(senders * count, DOF),
        previous_in.reshape(senders * count, RHS * DOF),
        strain_in.reshape(senders * count, RHS),
    )
    returned = (
        lax.all_to_all(
            new_rows.reshape(senders, count, RHS * DOF),
            "pool",
            split_axis=0,
            concat_axis=0,
            tiled=True,
        ),
        lax.all_to_all(
            for_sending(stress_rows.reshape(senders, count, RHS)),
            "pool",
            split_axis=0,
            concat_axis=0,
            tiled=True,
        ),
        lax.all_to_all(
            for_sending(tangent_rows.reshape(senders, count, RHS * RHS)),
            "pool",
            split_axis=0,
            concat_axis=0,
            tiled=True,
        ),
    )
    backward = placing.T
    weights = backward.astype(jnp.float32)
    new_flat = returned[0].reshape(groups * CAP, RHS * DOF)
    stress_flat = returned[1].reshape(groups * CAP, RHS)
    tangent_flat = returned[2].reshape(groups * CAP, RHS * RHS)
    fluct = jnp.dot(
        backward.astype(jnp.bfloat16), new_flat, preferred_element_type=jnp.float32
    ).astype(jnp.bfloat16)
    stress = jnp.dot(weights, stress_flat, precision=lax.Precision.HIGHEST)
    tangent = jnp.dot(weights, tangent_flat, precision=lax.Precision.HIGHEST)
    return (fluct, stress, tangent)


def solution(mesh):
    placed = (
        P("pool", "macro", None),
        P("pool", None, None),
        P(("macro", "pool"), None),
        P(("macro", "pool"), None),
        P(("macro", "pool"), None),
        P(("macro", "pool"), None),
    )
    return jax.shard_map(
        on_device,
        mesh=mesh,
        in_specs=placed,
        out_specs=(
            P(("macro", "pool"), None),
            P(("macro", "pool"), None),
            P(("macro", "pool"), None),
        ),
        check_vma=False,
    )
```

profile of v0, /device:TPU:0, one launch (start us, length us, event | category | flops | bytes accessed | tf_op | source)
XLA Modules:
  0.0 141.5 jit_solution(9060755702593379308)
XLA Ops:
  11.8 7.3 %all-to-all-start.3 = ((bf16[8,8,9]{2,1,0:T(8,128)(2,1)}), bf16[8,8,9]{2,1,0:T(8,128)(2,1)S(1)}, u32[]{:S(2)}, u32[]{:S(2)}) async-start(bf16[8,8,9]{2,1,0:T(8,128)(2,1)} %bitcast.8), calls=%async_computation.3 | async-start | bytes 32768 | tf_op jit(solution)/shard_map/all_to_all | solution.py:83
  19.1 1.8 %fusion.23 = bf16[8,8,768]{2,1,0:T(8,128)(2,1)} fusion(f32[64,768]{1,0:T(8,128)} %param.9, s32[64]{0:T(128)S(1)} %add_add_fusion), kind=kOutput, calls=%fused_computation.47 | convolution fusion | flops 37801984 | bytes 295168 | tf_op jit(solution)/shard_map/dot_general | solution.py:60
  20.9 4.8 %all-to-all-done.3 = bf16[8,8,9]{2,1,0:T(8,128)(2,1)S(1)} async-done(((bf16[8,8,9]{2,1,0:T(8,128)(2,1)}), bf16[8,8,9]{2,1,0:T(8,128)(2,1)S(1)}, u32[]{:S(2)}, u32[]{:S(2)}) %all-to-all-start.3) | async-done | bytes 1184 | tf_op jit(solution)/shard_map/all_to_all | solution.py:83
  25.6 3.4 %all-to-all-start.1 = ((bf16[8,8,768]{2,1,0:T(8,128)(2,1)}), bf16[8,8,768]{2,1,0:T(8,128)(2,1)S(1)}, u32[]{:S(2)}, u32[]{:S(2)}) async-start(bf16[8,8,768]{2,1,0:T(8,128)(2,1)} %fusion.23), calls=%async_computation.1 | async-start | bytes 196608 | tf_op jit(solution)/shard_map/all_to_all | solution.py:80
  30.3 5.7 %all-to-all-done.1 = bf16[8,8,768]{2,1,0:T(8,128)(2,1)S(1)} async-done(((bf16[8,8,768]{2,1,0:T(8,128)(2,1)}), bf16[8,8,768]{2,1,0:T(8,128)(2,1)S(1)}, u32[]{:S(2)}, u32[]{:S(2)}) %all-to-all-start.1) | async-done | bytes 98336 | tf_op jit(solution)/shard_map/all_to_all | solution.py:80
  36.1 3.6 %all-to-all-start = ((bf16[8,8,6912]{2,1,0:T(8,128)(2,1)}), bf16[8,8,6912]{2,1,0:T(8,128)(2,1)S(1)}, u32[]{:S(2)}, u32[]{:S(2)}) async-start(bf16[8,8,6912]{2,1,0:T(8,128)(2,1)} %fusion), calls=%async_computation | async-start | bytes 1769472 | tf_op jit(solution)/shard_map/all_to_all | solution.py:79
  39.8 19.9 %all-to-all-done = bf16[8,8,6912]{2,1,0:T(8,128)(2,1)S(1)} async-done(((bf16[8,8,6912]{2,1,0:T(8,128)(2,1)}), bf16[8,8,6912]{2,1,0:T(8,128)(2,1)S(1)}, u32[]{:S(2)}, u32[]{:S(2)}) %all-to-all-start) | async-done | bytes 884768 | tf_op jit(solution)/shard_map/all_to_all | solution.py:79
  59.7 1.4 reshape.109
  61.1 1.4 %bitcast_convert_fusion = f32[768,768]{1,0:T(8,128)S(1)} fusion(bf16[1,768,768]{2,1,0:T(8,128)(2,1)} %all-gather.2.cloned.1.call-done), kind=kLoop, calls=%fused_computation.45 | loop fusion | flops 589824 | bytes 3538944 | tf_op jit(solution)/shard_map/convert_element_type | solution.py:24
  62.6 6.5 %gather_fusion = f32[768]{0:T(1024)S(1)} fusion(f32[768,768]{1,0:T(8,128)S(1)} %bitcast_convert_fusion, s32[768]{0:T(1024)S(1)} %or_reduce_fusion), kind=kCustom, calls=%fused_computation | custom fusion | bytes 12288 | tf_op jit(solution)/shard_map/jit(diagonal)/cond/branch_0_fun/gather | solution.py:25
  69.1 3.5 %fusion.7 = f32[64,9,768]{2,0,1:T(8,128)S(1)} fusion(bf16[1,768,768]{2,1,0:T(8,128)(2,1)} %all-gather.2.cloned.1.call-done, f32[64,768]{1,0:T(8,128)S(1)} %bitcast_convert_fusion.1, f32[9,768]{1,0:T(8,128)S(1)} %bitcast.60, bf16[64,9,768]{2,1,0:T(8,128)(2,1)} %reshape.109), kind=kOutput, calls=%fused_computation.23 | convolution fusion | flops 681246720 | bytes 4058112 | tf_op jit(solution)/shard_map/dot_general | solution.py:29
  72.6 2.6 %fusion.5 = (f32[64,9]{0,1:T(8,128)S(1)}, f32[64,9]{0,1:T(8,128)S(1)}, f32[64,9,768]{2,0,1:T(8,128)S(1)}) fusion(f32[64,9,768]{2,0,1:T(8,128)S(1)} %fusion.7, f32[768]{0:T(1024)S(1)} %broadcast_divide_fusion, f32[64,768]{1,0:T(8,128)S(1)} %bitcast_convert_fusion.1, bf16[1,768,768]{2,1,0:T(8,128)(2,1)S(1)} %copy-done.2), kind=kOutput, calls=%fused_computation.21 | convolution fusion | flops 4080401408 | bytes 4922880 | tf_op jit(solution)/shard_map/dot_general | solution.py:29
  75.7 3.1 %multiply_reduce_fusion.2 = (f32[64,9]{0,1:T(8,128)S(1)}, f32[64,9,768]{2,0,1:T(8,128)S(1)}) fusion(f32[64,768]{1,0:T(8,128)S(1)} %bitcast_convert_fusion.1, f32[64,9,768]{2,0,1:T(8,128)S(1)} %fusion.7, f32[64,9]{0,1:T(8,128)S(1)} %add_divide_fusion.5, f32[64,9,768]{2,0,1:T(8,128)S(1)} %get-tuple-element.11, f32[64,9]{0,1:T(8,128)S(1)} %add_divide_fusion.6, ...), kind=kOutput, calls=%fused_computation.35 | convolution fusion | flops 4083940864 | bytes 6694656 | tf_op jit(solution)/shard_map/dot_general | solution.py:29
  80.4 2.5 %multiply_reduce_fusion.1 = (f32[64,9]{0,1:T(8,128)S(1)}, f32[64,9,768]{2,0,1:T(8,128)S(1)}) fusion(f32[64,9,768]{2,0,1:T(8,128)S(1)} %multiply_add_fusion.1, f32[64,768]{1,0:T(8,128)S(1)} %bitcast_convert_fusion.1, bf16[1,768,768]{2,1,0:T(8,128)(2,1)S(1)} %copy-done.2), kind=kOutput, calls=%fused_computation.32 | convolution fusion | flops 4078632448 | bytes 4917504 | tf_op jit(solution)/shard_map/dot_general | solution.py:29
  83.5 3.0 %multiply_reduce_fusion = f32[64,9]{0,1:T(8,128)S(1)} fusion(f32[64,9,768]{2,0,1:T(8,128)S(1)} %multiply_add_fusion.1, f32[64,9,768]{2,0,1:T(8,128)S(1)} %get-tuple-element.8, bf16[1,768,768]{2,1,0:T(8,128)(2,1)S(1)} %copy-done.2, f32[64,9]{0,1:T(8,128)S(1)} %add_divide_fusion.1, f32[768]{0:T(1024)S(1)} %broadcast_divide_fusion, ...), kind=kOutput, calls=%fused_computation.30 | convolution fusion | flops 4081286656 | bytes 4922880 | tf_op jit(solution)/shard_map/dot_general | solution.py:29
  86.6 1.4 %fusion.40 = (bf16[64,9,768]{2,0,1:T(8,128)(2,1)S(1)}, f32[64,9,768]{2,0,1:T(8,128)S(1)}) fusion(f32[64,9,768]{2,0,1:T(8,128)S(1)} %multiply_add_fusion.1, f32[64,9]{0,1:T(8,128)S(1)} %add_divide_fusion.1, f32[64,9,768]{2,0,1:T(8,128)S(1)} %get-tuple-element.8, f32[64,9]{0,1:T(8,128)S(1)} %add_divide_fusion, f32[64,9]{0,1:T(8,128)S(1)} %add_divide_fusion.2, ...), kind=kLoop, calls=%fused_computation.84 | loop fusion | flops 8404992 | bytes 10633728 | tf_op jit(solution)/shard_map/convert_element_type | solution.py:49
  88.0 2.1 %multiply_reduce_fusion.3 = (bf16[64,9]{0,1:T(8,128)(2,1)S(1)}, bf16[64,9,9]{0,2,1:T(8,128)(2,1)S(1)}) fusion(f32[64,9]{0,1:T(8,128)S(1)} %convert.3, f32[64,9,768]{2,0,1:T(8,128)S(1)} %get-tuple-element.6, f32[1,9,768]{2,0,1:T(1,128)S(1)} %copy-done.3), kind=kOutput, calls=%fused_computation.56 | convolution fusion | flops 47795904 | bytes 1810944 | tf_op jit(solution)/shard_map/sik,jk->sij/dot_general | solution.py:46
  90.9 3.4 %all-to-all-start.4 = ((bf16[8,8,9]{2,1,0:T(8,128)(2,1)}), bf16[8,8,9]{2,1,0:T(8,128)(2,1)S(1)}, u32[]{:S(2)}, u32[]{:S(2)}) async-start(bf16[8,8,9]{2,1,0:T(8,128)(2,1)} %bitcast.44), calls=%async_computation.4 | async-start | bytes 32768 | tf_op jit(solution)/shard_map/all_to_all | solution.py:103
  95.2 5.6 %all-to-all-done.4 = bf16[8,8,9]{2,1,0:T(8,128)(2,1)S(1)} async-done(((bf16[8,8,9]{2,1,0:T(8,128)(2,1)}), bf16[8,8,9]{2,1,0:T(8,128)(2,1)S(1)}, u32[]{:S(2)}, u32[]{:S(2)}) %all-to-all-start.4) | async-done | bytes 1184 | tf_op jit(solution)/shard_map/all_to_all | solution.py:103
  100.9 3.3 %all-to-all-start.5 = ((bf16[8,8,81]{2,1,0:T(8,128)(2,1)}), bf16[8,8,81]{2,1,0:T(8,128)(2,1)S(1)}, u32[]{:S(2)}, u32[]{:S(2)}) async-start(bf16[8,8,81]{2,1,0:T(8,128)(2,1)} %copy.18), calls=%async_computation.5 | async-start | bytes 32768 | tf_op jit(solution)/shard_map/all_to_all | solution.py:110
  106.0 4.7 %all-to-all-done.5 = bf16[8,8,81]{2,1,0:T(8,128)(2,1)S(1)} async-done(((bf16[8,8,81]{2,1,0:T(8,128)(2,1)}), bf16[8,8,81]{2,1,0:T(8,128)(2,1)S(1)}, u32[]{:S(2)}, u32[]{:S(2)}) %all-to-all-start.5) | async-done | bytes 10400 | tf_op jit(solution)/shard_map/all_to_all | solution.py:110
  110.7 3.6 %all-to-all-start.2 = ((bf16[8,8,6912]{2,1,0:T(8,128)(2,1)}), bf16[8,8,6912]{2,1,0:T(8,128)(2,1)S(1)}, u32[]{:S(2)}, u32[]{:S(2)}) async-start(bf16[8,8,6912]{2,1,0:T(8,128)(2,1)} %reshape_reshape.2), calls=%async_computation.2 | async-start | bytes 1769472 | tf_op jit(solution)/shard_map/all_to_all | solution.py:96
  115.9 17.4 %all-to-all-done.2 = bf16[8,8,6912]{2,1,0:T(8,128)(2,1)S(1)} async-done(((bf16[8,8,6912]{2,1,0:T(8,128)(2,1)}), bf16[8,8,6912]{2,1,0:T(8,128)(2,1)S(1)}, u32[]{:S(2)}, u32[]{:S(2)}) %all-to-all-start.2) | async-done | bytes 884768 | tf_op jit(solution)/shard_map/all_to_all | solution.py:96
  133.3 1.4 convolution_convert_fusion
  (42 shorter events, 13.9 us)
Async XLA Ops:
  7.2 21.8 %copy-start = (bf16[64,6912]{1,0:T(8,128)(2,1)S(1)}, bf16[64,6912]{1,0:T(8,128)(2,1)}, u32[]{:S(2)}) copy-start(bf16[64,6912]{1,0:T(8,128)(2,1)} %param.11) | copy-start | bytes 2654212
  7.2 53.9 %all-gather.2.cloned.1.call-start = ((), (), s32[]{:S(2)}) async-start(), calls=%async_computation.6 | async-start | bytes 1474560 | tf_op jit(solution)/shard_map/all_gather | solution.py:66
  11.8 13.8 %all-to-all-start.3 = ((bf16[8,8,9]{2,1,0:T(8,128)(2,1)}), bf16[8,8,9]{2,1,0:T(8,128)(2,1)S(1)}, u32[]{:S(2)}, u32[]{:S(2)}) async-start(bf16[8,8,9]{2,1,0:T(8,128)(2,1)} %bitcast.8), calls=%async_computation.3 | async-start | bytes 32768 | tf_op jit(solution)/shard_map/all_to_all | solution.py:83
  25.6 10.4 %all-to-all-start.1 = ((bf16[8,8,768]{2,1,0:T(8,128)(2,1)}), bf16[8,8,768]{2,1,0:T(8,128)(2,1)S(1)}, u32[]{:S(2)}, u32[]{:S(2)}) async-start(bf16[8,8,768]{2,1,0:T(8,128)(2,1)} %fusion.23), calls=%async_computation.1 | async-start | bytes 196608 | tf_op jit(solution)/shard_map/all_to_all | solution.py:80
  29.0 10.6 %copy-start.3 = (f32[1,9,768]{2,0,1:T(1,128)S(1)}, f32[1,9,768]{2,0,1:T(1,128)}, u32[]{:S(2)}) copy-start(f32[1,9,768]{2,0,1:T(1,128)} %param.7) | copy-start | bytes 82948
  36.1 23.6 %all-to-all-start = ((bf16[8,8,6912]{2,1,0:T(8,128)(2,1)}), bf16[8,8,6912]{2,1,0:T(8,128)(2,1)S(1)}, u32[]{:S(2)}, u32[]{:S(2)}) async-start(bf16[8,8,6912]{2,1,0:T(8,128)(2,1)} %fusion), calls=%async_computation | async-start | bytes 1769472 | tf_op jit(solution)/shard_map/all_to_all | solution.py:79
  69.1 3.5 %copy-start.2 = (bf16[1,768,768]{2,1,0:T(8,128)(2,1)S(1)}, bf16[1,768,768]{2,1,0:T(8,128)(2,1)}, u32[]{:S(2)}) copy-start(bf16[1,768,768]{2,1,0:T(8,128)(2,1)} %all-gather.2.cloned.1.call-done) | copy-start | bytes 3538948
  83.5 3.0 %copy-start.1 = (bf16[64,9,768]{2,1,0:T(8,128)(2,1)S(1)}, bf16[64,9,768]{2,1,0:T(8,128)(2,1)}, u32[]{:S(2)}) copy-start(bf16[64,9,768]{2,1,0:T(8,128)(2,1)} %reshape.109) | copy-start | bytes 2654212
  90.9 10.0 %all-to-all-start.4 = ((bf16[8,8,9]{2,1,0:T(8,128)(2,1)}), bf16[8,8,9]{2,1,0:T(8,128)(2,1)S(1)}, u32[]{:S(2)}, u32[]{:S(2)}) async-start(bf16[8,8,9]{2,1,0:T(8,128)(2,1)} %bitcast.44), calls=%async_computation.4 | async-start | bytes 32768 | tf_op jit(solution)/shard_map/all_to_all | solution.py:103
  100.9 9.9 %all-to-all-start.5 = ((bf16[8,8,81]{2,1,0:T(8,128)(2,1)}), bf16[8,8,81]{2,1,0:T(8,128)(2,1)S(1)}, u32[]{:S(2)}, u32[]{:S(2)}) async-start(bf16[8,8,81]{2,1,0:T(8,128)(2,1)} %copy.18), calls=%async_computation.5 | async-start | bytes 32768 | tf_op jit(solution)/shard_map/all_to_all | solution.py:110
  110.7 22.6 %all-to-all-start.2 = ((bf16[8,8,6912]{2,1,0:T(8,128)(2,1)}), bf16[8,8,6912]{2,1,0:T(8,128)(2,1)S(1)}, u32[]{:S(2)}, u32[]{:S(2)}) async-start(bf16[8,8,6912]{2,1,0:T(8,128)(2,1)} %reshape_reshape.2), calls=%async_computation.2 | async-start | bytes 1769472 | tf_op jit(solution)/shard_map/all_to_all | solution.py:96
Sparse Core Ops, SparseCore 0:
  9.6 20.1 all-gather.1
where the time goes:
time: 142 us
  waiting for transfers between devices  58.9 us (41%)
  starting transfers between devices  24.5 us (17%)
  matrix products  23.6 us (17%)
  between operations  14.3 us (10%)
  local copies, waits for them, and re-layouts  12.2 us (9%)
  other arithmetic  8.01 us (6%)
    all_to_all x1, waiting for transfers between devices, on_device(): lax.all_to_all(send_previous, 'pool', split_axis=0, concat_axis=0, tiled=...  19.9 us
    all_to_all x1, waiting for transfers between devices, on_device(): lax.all_to_all(new_rows.reshape(senders, count, RHS * DOF), 'pool', split...  17.4 us
    dot_general x5, matrix products, apply_stiffness(): jnp.dot(flat, stiff, precision=lax.Precision.HIGHEST)  14.7 us
    all_to_all x1, starting transfers between devices, on_device(): lax.all_to_all(send_strain.astype(jnp.bfloat16), 'pool', split_axis=0, co...  7.25 us
    gather x1, local copies, waits for them, and re-layouts, solve_cells(): inverse = 1.0 / jnp.diagonal(stiff)  6.48 us
    all_to_all x1, waiting for transfers between devices, on_device(): lax.all_to_all(send_contact.astype(jnp.bfloat16), 'pool', split_axis=0, c...  5.75 us
    all_to_all x1, waiting for transfers between devices, on_device(): lax.all_to_all(for_sending(stress_rows.reshape(senders, count, RHS)), 'po...  5.64 us
    all_to_all x1, waiting for transfers between devices, on_device(): lax.all_to_all(send_strain.astype(jnp.bfloat16), 'pool', split_axis=0, co...  4.78 us
  transfers between devices with their start and end apart: 7, of which 6 were waited for; matrix products, arithmetic and copies ran while one was open for 9% of the time, Pallas kernels for 0%

commit v1 on v0

v1 whole, which is shorter than its diff:
```python
import functools
import itertools
import math

import jax
import jax.numpy as jnp
from jax import lax
from jax.experimental import pallas as pl
from jax.experimental.pallas import tpu as pltpu
from jax.sharding import PartitionSpec as P

ITERS = 4
CAP = 8
LANES = 128
PACK = 16
CORES = 2
BF = jnp.bfloat16
F32 = jnp.float32


def split_pool(pool):
    fast = max(d for d in range(1, pool + 1) if pool % d == 0 and d * d <= pool)
    return pool // fast, fast


def half_plan(dof, macro):
    rows = dof // macro
    unit = math.gcd(rows, LANES)
    blocks = dof // LANES
    per = LANES // unit
    fixed = [(r, (r + k) % blocks) for r in range(blocks) for k in range((blocks - 1) // 2 + 1)]
    open_pairs = [(r, r + blocks // 2) for r in range(blocks // 2)] if blocks % 2 == 0 else []
    best = None
    for turned in itertools.product((0, 1), repeat=len(open_pairs)):
        chosen = fixed + [(b, a) if t else (a, b) for t, (a, b) in zip(turned, open_pairs)]
        lists = [[] for _ in range(macro)]
        for r, c in sorted(chosen):
            for q in range(per):
                stripe = r * per + q
                lists[stripe * unit // rows].append((stripe, c))
        most = max(len(each) for each in lists)
        if best is None or most < best[0]:
            best = (most, lists, chosen)
    return unit, best[0], best[1], [(r, c) for r, c in best[2] if r != c]


def by_distance(n):
    return [sorted(range(n), key=lambda s: (abs(s - p), s)) for p in range(n)]


def pick(table, at, k):
    out = jnp.int32(table[0][k])
    for p in range(1, len(table)):
        out = jnp.where(at == p, jnp.int32(table[p][k]), out)
    return out


def kernel(sizes, panel_ref, loads_ref, family_ref, contact_ref, strain_ref, previous_ref,
           fluct_ref, stress_ref, tangent_ref,
           held, whole, load, slot_prev, slot_contact, slot_strain, slot_out, slot_small,
           iterate, residual, direction, inverse_ref, send_sem, recv_sem):
    macro, pool, plan, cut = sizes
    unit, most, lists, mirrored = plan
    count, dof = loads_ref.shape[1], loads_ref.shape[2]
    rows = panel_ref.shape[1]
    points = family_ref.shape[0]
    slots = pool * CAP
    blocks = dof // LANES
    nz, nx = split_pool(pool)
    ny = macro // CORES
    total_rows = held.shape[2]
    cuts = ((0, cut), (cut, total_rows - cut))

    my_macro, my_pool = lax.axis_index("macro"), lax.axis_index("pool")
    pz, px = my_pool // nx, my_pool % nx
    py, pc = my_macro // CORES, my_macro % CORES
    here = (pz, px, py)
    extent = (nz, nx, ny)
    orders = tuple(by_distance(n) for n in extent)

    def device(at, core):
        z, x, y = at
        return (y * CORES + core, z * nx + x)

    def moved(axis, to):
        return tuple(to if a == axis else here[a] for a in range(3))

    barrier = pltpu.get_barrier_semaphore()
    pl.semaphore_signal(barrier, inc=1, device_id=device(here, 1 - pc), device_id_type=pl.DeviceIdType.MESH)
    expected = jnp.int32(1)
    for axis in range(3):
        for by in (-1, 1):
            to = here[axis] + by
            ok = jnp.logical_and(to >= 0, to < extent[axis])
            expected = expected + ok.astype(jnp.int32)

            @pl.when(ok)
            def _(axis=axis, to=to):
                pl.semaphore_signal(
                    barrier, inc=1, device_id=device(moved(axis, to), pc), device_id_type=pl.DeviceIdType.MESH)

    for m in range(macro):

        @pl.when(my_macro == m)
        def _(m=m):
            for t, (stripe, c) in enumerate(lists[m]):
                low = stripe * unit - m * rows
                held[m, my_pool, t * unit:(t + 1) * unit, :] = panel_ref[
                    0, low:low + unit, c * LANES:(c + 1) * LANES]
            for t, b in enumerate(range(m, blocks, macro)):
                part = loads_ref[0, :, b * LANES:(b + 1) * LANES]
                part = jnp.concatenate([part, jnp.zeros((PACK - count, LANES), F32)], axis=0)
                low = most * unit + t * PACK
                held[m, my_pool, low:low + PACK, :] = part.astype(BF)

    pl.semaphore_wait(barrier, expected)
    pending = []

    def copy_of(src, h, to, core, sem):
        m, p = src
        start, size = cuts[h]
        view = held.at[m, p, pl.ds(start, size), :]
        return pltpu.make_async_remote_copy(
            src_ref=view, dst_ref=view, send_sem=send_sem.at[sem], recv_sem=recv_sem.at[m, p, h],
            device_id=device(to, core), device_id_type=pl.DeviceIdType.MESH)

    def start(src, h, to, core, cond):
        copy = copy_of(src, h, to, core, len(pending))
        pending.append((copy, cond))
        if cond is None:
            copy.start()
        else:
            pl.when(cond)(copy.start)

    def arrive(src, h):
        copy_of(src, h, here, 1 - pc, 0).wait_recv()

    def along(src, h, axis, k, source):
        n, p = extent[axis], here[axis]
        if n == 1 or (k > 0 and n == 2):
            return
        if k == 0 and n == 2:
            start(src, h, moved(axis, 1 - p), pc, None)
        elif k == 0:
            for by in (1, -1):
                to = p + by
                start(src, h, moved(axis, to), pc, jnp.logical_and(to >= 0, to < n))
        else:
            to = jnp.where(p > source, p + 1, p - 1)
            start(src, h, moved(axis, to), pc, jnp.logical_and(to >= 0, to < n))

    paths = ((0, 1, 2), (0, 2, 1))

    def sources(ks):
        return tuple(here[a] if ks[a] == 0 else pick(orders[a], here[a], ks[a]) for a in range(3))

    def event(ks, h):
        at = sources(ks)
        src = device(at, pc)
        if any(ks):
            arrive(src, h)
        path = paths[h]
        last = max([i for i in range(3) if ks[path[i]]], default=0)
        for i in range(last, 3):
            along(src, h, path[i], ks[path[i]], at[path[i]])
        start(src, h, here, 1 - pc, None)

    def event_z(kz):
        for h in (0, 1):
            event((kz, 0, 0), h)

    def event_xy(kz):
        for k in range(1, nx):
            event((kz, k, 0), 0)
        for k in range(1, ny):
            event((kz, 0, k), 1)
        for kx in range(nx):
            for ky in range(1, ny):
                event((kz, kx, ky), 0)
        for ky in range(ny):
            for kx in range(1, nx):
                event((kz, kx, ky), 1)

    def sibling(kz):
        for kx in range(nx):
            for ky in range(ny):
                at = sources((kz, kx, ky))
                for h in (0, 1):
                    arrive(device(at, 1 - pc), h)

    event_z(0)

    family = family_ref[...]
    named = family == lax.broadcasted_iota(jnp.int32, (points, pool), 1)
    row_at = lax.broadcasted_iota(jnp.int32, (points, points), 0)
    col_at = lax.broadcasted_iota(jnp.int32, (points, points), 1)
    before = jnp.dot((col_at < row_at).astype(BF), named.astype(BF), preferred_element_type=F32)
    rank = jnp.sum(jnp.where(named, before, 0.0), axis=1, keepdims=True)
    slot = family * CAP + rank.astype(jnp.int32)
    slot_row = jnp.sum(jnp.where(row_at == col_at, slot.astype(F32), 0.0), axis=0, keepdims=True).astype(jnp.int32)
    placing = (lax.broadcasted_iota(jnp.int32, (slots, points), 0) == slot_row).astype(BF)
    taking = (slot == lax.broadcasted_iota(jnp.int32, (points, slots), 1)).astype(BF)

    def parts3(value):
        high = value.astype(BF)
        rest = value - high.astype(F32)
        middle = rest.astype(BF)
        return high, middle, (rest - middle.astype(F32)).astype(BF)

    def move3(matrix, value):
        return sum(jnp.dot(matrix, part, preferred_element_type=F32) for part in parts3(value))

    for i in range(count):
        span = slice(i * dof, (i + 1) * dof)
        slot_prev[:, span] = jnp.dot(placing, previous_ref[:, span], preferred_element_type=F32).astype(BF)
    slot_contact[...] = move3(placing, contact_ref[...])
    slot_strain[...] = move3(placing, strain_ref[...])

    eye = (lax.broadcasted_iota(jnp.int32, (LANES, LANES), 0)
           == lax.broadcasted_iota(jnp.int32, (LANES, LANES), 1))

    def assemble(j, f):
        for m in range(macro):
            for t, (stripe, c) in enumerate(lists[m]):
                whole[j, stripe * unit:(stripe + 1) * unit, c * LANES:(c + 1) * LANES] = held[
                    m, f, t * unit:(t + 1) * unit, :]
            for t, b in enumerate(range(m, blocks, macro)):
                low = most * unit + t * PACK
                load[j, :, b * LANES:(b + 1) * LANES] = held[m, f, low:low + PACK, :]
        for r, c in mirrored:
            block = whole[j, r * LANES:(r + 1) * LANES, c * LANES:(c + 1) * LANES]
            whole[j, c * LANES:(c + 1) * LANES, r * LANES:(r + 1) * LANES] = block.T
        for r in range(blocks):
            span = slice(r * LANES, (r + 1) * LANES)
            diagonal = jnp.sum(jnp.where(eye, whole[j, span, span].astype(F32), 0.0), axis=0, keepdims=True)
            inverse_ref[j, :, span] = 1.0 / diagonal

    def solve_pair(pair):
        at16 = pl.ds(pl.multiple_of(pair * 2 * CAP, 2 * CAP), 2 * CAP)
        for j in (0, 1):
            assemble(j, pair * 2 + j)
        for i in range(count):
            both = slot_prev[at16, i * dof:(i + 1) * dof].astype(F32)
            iterate[0, i * CAP:(i + 1) * CAP, :] = both[:CAP]
            iterate[1, i * CAP:(i + 1) * CAP, :] = both[CAP:]

        def contact_of(j):
            return slot_contact[pl.ds(pl.multiple_of(pair * 2 * CAP + j * CAP, CAP), CAP), :]

        def apply(j, field):
            product = jnp.dot(field.astype(BF), whole[j], preferred_element_type=F32)
            extra = contact_of(j)[None, :, :] * field.reshape(count, CAP, dof)
            return product + extra.reshape(count * CAP, dof)

        current = []
        for j in (0, 1):
            loads = load[j, 0:count, :].astype(F32)
            wide = jnp.broadcast_to(loads[:, None, :], (count, CAP, dof)).reshape(count * CAP, dof)
            left = wide - apply(j, iterate[j])
            scaled = inverse_ref[j] * left
            residual[j] = left
            direction[j] = scaled
            current.append(jnp.sum(left * scaled, axis=-1, keepdims=True))

        def sweep(_, current):
            after = []
            for j in (0, 1):
                toward = direction[j]
                image = apply(j, toward)
                step = current[j] / (jnp.sum(toward * image, axis=-1, keepdims=True) + 1e-6)
                iterate[j] = iterate[j] + step * toward
                left = residual[j] - step * image
                scaled = inverse_ref[j] * left
                updated = jnp.sum(left * scaled, axis=-1, keepdims=True)
                residual[j] = left
                direction[j] = scaled + (updated / (current[j] + 1e-6)) * toward
                after.append(updated)
            return tuple(after)

        lax.fori_loop(0, ITERS, sweep, tuple(current))

        for i in range(count):
            span = slice(i * CAP, (i + 1) * CAP)
            both = jnp.concatenate([iterate[0, span, :], iterate[1, span, :]], axis=0)
            slot_out[at16, i * dof:(i + 1) * dof] = both.astype(BF)
        for j in (0, 1):
            mine = pl.ds(pl.multiple_of(pair * 2 * CAP + j * CAP, CAP), CAP)
            value = iterate[j]
            high = value.astype(BF)
            low = (value - high.astype(F32)).astype(BF)
            weights = load[j]
            contract = (((1,), (1,)), ((), ()))
            tang = (lax.dot_general(high, weights, contract, preferred_element_type=F32)
                    + lax.dot_general(low, weights, contract, preferred_element_type=F32)) * (1.0 / dof)
            strain = slot_strain[mine, :]
            for i in range(count):
                piece = tang[i * CAP:(i + 1) * CAP, 0:count]
                slot_small[mine, i * count:(i + 1) * count] = piece
                slot_small[mine, count * count + i:count * count + i + 1] = jnp.sum(
                    piece * strain, axis=-1, keepdims=True)

    def solve(kz):
        at = pick(orders[0], pz, kz) if kz else pz
        for q in range(nx // 2):
            solve_pair(at * (nx // 2) + q)

    for kz in range(nz):
        if kz + 1 < nz:
            event_z(kz + 1)
        event_xy(kz)
        sibling(kz)
        solve(kz)

    for i in range(count):
        span = slice(i * dof, (i + 1) * dof)
        fluct_ref[:, span] = jnp.dot(taking, slot_out[:, span], preferred_element_type=F32).astype(BF)
    small = move3(taking, slot_small[...])
    tangent_ref[...] = small[:, 0:count * count]
    stress_ref[...] = small[:, count * count:count * count + count]

    for copy, cond in pending:
        if cond is None:
            copy.wait_send()
        else:
            pl.when(cond)(copy.wait_send)


def count_sends(nz, nx, ny):
    def along(n, k):
        if n == 1 or (k > 0 and n == 2):
            return 0
        return 1 if n == 2 or k > 0 else 2

    total = 0
    for path in ((0, 1, 2), (0, 2, 1)):
        for ks in itertools.product(range(nz), range(nx), range(ny)):
            last = max([i for i in range(3) if ks[path[i]]], default=0)
            total += 1 + sum(along((nz, nx, ny)[path[i]], ks[path[i]]) for i in range(last, 3))
    return total


def on_device(macro, pool, panels, loads, family, contact, strain, previous):
    points, dof = contact.shape
    count = strain.shape[1]
    plan = half_plan(dof, macro)
    unit, most = plan[0], plan[1]
    shares = -(-(dof // LANES) // macro)
    total_rows = most * unit + shares * PACK
    cut = -(-total_rows // (2 * PACK)) * PACK
    slots = pool * CAP
    nz, nx = split_pool(pool)
    vmem = pl.BlockSpec(memory_space=pltpu.VMEM)
    return pl.pallas_call(
        functools.partial(kernel, (macro, pool, plan, cut)),
        out_shape=(
            jax.ShapeDtypeStruct(previous.shape, BF),
            jax.ShapeDtypeStruct((points, count), F32),
            jax.ShapeDtypeStruct((points, count * count), F32),
        ),
        in_specs=[vmem] * 6,
        out_specs=(vmem,) * 3,
        scratch_shapes=[
            pltpu.VMEM((macro, pool, total_rows, LANES), BF),
            pltpu.VMEM((2, dof, dof), BF),
            pltpu.VMEM((2, PACK, dof), BF),
            pltpu.VMEM((slots, count * dof), BF),
            pltpu.VMEM((slots, dof), F32),
            pltpu.VMEM((slots, count), F32),
            pltpu.VMEM((slots, count * dof), BF),
            pltpu.VMEM((slots, LANES), F32),
            pltpu.VMEM((2, count * CAP, dof), F32),
            pltpu.VMEM((2, count * CAP, dof), F32),
            pltpu.VMEM((2, count * CAP, dof), F32),
            pltpu.VMEM((2, 1, dof), F32),
            pltpu.SemaphoreType.DMA((count_sends(nz, nx, macro // CORES),)),
            pltpu.SemaphoreType.DMA((macro, pool, 2)),
        ],
        compiler_params=pltpu.CompilerParams(
            collective_id=0, has_side_effects=True, vmem_limit_bytes=56 * 1024 * 1024),
    )(panels, loads, family, contact, strain, previous)


def solution(mesh):
    placed = (
        P("pool", "macro", None),
        P("pool", None, None),
        P(("macro", "pool"), None),
        P(("macro", "pool"), None),
        P(("macro", "pool"), None),
        P(("macro", "pool"), None),
    )
    return jax.shard_map(
        functools.partial(on_device, mesh.shape["macro"], mesh.shape["pool"]),
        mesh=mesh,
        in_specs=placed,
        out_specs=(
            P(("macro", "pool"), None),
            P(("macro", "pool"), None),
            P(("macro", "pool"), None),
        ),
        check_vma=False,
    )
```

time: 142 us -> 74.7 us (0.53)
  Pallas kernels: 0 us -> 66.7 us
  waiting for transfers between devices: 58.9 us -> 0 us
  starting transfers between devices: 24.5 us -> 0 us
  matrix products: 23.6 us -> 0 us
  between operations: 14.3 us -> 0.65 us
  other arithmetic: 8.01 us -> 0 us
  local copies, waits for them, and re-layouts: 12.2 us -> 6.93 us
    pallas_call x0 -> x1, Pallas kernels: none -> 66.7 us  [on_device(): pl.pallas_call(functools.partial(kernel, (macro, pool, plan, cut)), out_s...]
    all_to_all x6 -> x0, waiting for transfers between devices: 58.2 us -> none  [the longest x1 19.9 us: on_device(): lax.all_to_all(send_previous, 'pool', split_axis=0, concat_axis=0, tiled=...]
    all_to_all x6 -> x0, starting transfers between devices: 24.5 us -> none  [the longest x1 7.25 us: on_device(): lax.all_to_all(send_strain.astype(jnp.bfloat16), 'pool', split_axis=0, co...]
    dot_general x12 -> x0, matrix products: 23.6 us -> none  [the longest x5 14.7 us: apply_stiffness(): jnp.dot(flat, stiff, precision=lax.Precision.HIGHEST)]
    gather x1 -> x0, local copies, waits for them, and re-layouts: 6.48 us -> none  [solve_cells(): inverse = 1.0 / jnp.diagonal(stiff)]
    unnamed x10 -> x11, local copies, waits for them, and re-layouts: 0.1 us -> 5.5 us
    convert_element_type x3 -> x0, other arithmetic: 3.62 us -> none  [the longest x1 1.45 us: solve_cells(): iterate.astype(jnp.bfloat16).reshape(cells, count * width)]
    reduce_sum x4 -> x0, other arithmetic: 2.83 us -> none  [the longest x3 2 us: solve_cells(): updated = jnp.sum(residual * scaled, axis=-1)]
  transfers between devices with their start and end apart: 7 -> 0, of which waited for: 6 -> 0; matrix products, arithmetic and copies ran while one was open for 9% -> 0% of each run, Pallas kernels for 0% -> 0%
where the time goes in v1:
time: 74.7 us; the launch traced here: 74.3 us
  Pallas kernels  66.7 us (89%)
  local copies, waits for them, and re-layouts  6.93 us (9%)
    pallas_call x1, Pallas kernels, on_device(): pl.pallas_call(functools.partial(kernel, (macro, pool, plan, cut)), out_s...  66.7 us
    unnamed x11, local copies, waits for them, and re-layouts  5.5 us

profile of v1, /device:TPU:0, one launch (start us, length us, event | category | flops | bytes accessed | tf_op | source)
XLA Modules:
  0.0 74.3 jit_solution(8680585418990843635)
XLA Ops:
  0.6 0.0 copy-start.2
  0.6 1.4 %copy.10.family_ref = s32[64,1]{1,0:T(8,128)} copy(s32[64,1]{0,1:T(1,128)} %param.8) | data formatting | bytes 512 | tf_op args[2]
  2.0 0.0 copy-done.2
  2.0 0.0 copy-start.1
  2.0 0.7 copy.11.strain_ref
  2.7 0.1 copy-done.1
  2.8 0.6 copy.9.loads_ref
  3.4 66.7 %shard_map.85 = (bf16[64,6912]{1,0:T(8,128)(2,1)}, f32[64,9]{1,0:T(8,128)}, f32[64,81]{1,0:T(8,128)}) custom-call(bf16[1,192,768]{2,1,0:T(8,128)(2,1)} %panel_ref.1, f32[1,9,768]{2,1,0:T(8,128)} %copy.9.loads_ref, s32[64,1]{1,0:T(8,128)} %copy.10.family_ref, f32[64,768]{1,0:T(8,128)} %contact_ref.1, f32[64,9]{1,0:T(8,128)} %copy.11.strain_ref, ...), custom_call_target="tpu_custom_call" | custom-call | tf_op jit(solution)/shard_map/pallas_call | solution.py:353
  70.1 1.4 %copy.12 = f32[64,9]{0,1:T(8,128)} copy(f32[64,9]{1,0:T(8,128)} %get-tuple-element.4) | data formatting | bytes 4608 | tf_op jit(solution)/shard_map/pallas_call | solution.py:353
  71.6 0.0 copy-start
  71.6 2.1 %copy.15 = bf16[64,6912]{1,0:T(8,128)(2,1)} copy(bf16[64,6912]{1,0:T(8,128)(2,1)} %get-tuple-element.9) | data formatting | bytes 1769472
  73.7 0.0 copy-done
  73.7 0.6 copy.16
Async XLA Ops:
  0.6 1.4 %copy-start.2 = (f32[64,9]{0,1:T(8,128)S(1)}, f32[64,9]{0,1:T(8,128)}, u32[]{:S(2)}) copy-start(f32[64,9]{0,1:T(8,128)} %param.10) | copy-start | bytes 6916
  2.0 0.7 %copy-start.1 = (f32[1,9,768]{2,0,1:T(1,128)S(1)}, f32[1,9,768]{2,0,1:T(1,128)}, u32[]{:S(2)}) copy-start(f32[1,9,768]{2,0,1:T(1,128)} %param.7) | copy-start | bytes 82948
  71.6 2.1 %copy-start = (f32[64,81]{1,0:T(8,128)S(1)}, f32[64,81]{1,0:T(8,128)}, u32[]{:S(2)}) copy-start(f32[64,81]{1,0:T(8,128)} %get-tuple-element.11) | copy-start | bytes 62212

commit v2 on v1

--- a/solution.py
+++ b/solution.py
@@ -55,15 +55,55 @@
     return out
 
 
+NT = (((1,), (1,)), ((), ()))
+
+
+def parts3(value):
+    high = value.astype(BF)
+    rest = value - high.astype(F32)
+    middle = rest.astype(BF)
+    return high, middle, (rest - middle.astype(F32)).astype(BF)
+
+
+def slots_of(family_row, pool):
+    points = family_row.shape[1]
+    row_at = lax.broadcasted_iota(jnp.int32, (points, points), 0)
+    col_at = lax.broadcasted_iota(jnp.int32, (points, points), 1)
+    eye = row_at == col_at
+    wide = jnp.broadcast_to(family_row.astype(F32), (points, points))
+    family = jnp.sum(jnp.where(eye, wide, 0.0), axis=1, keepdims=True).astype(jnp.int32)
+    earlier = jnp.logical_and(wide.astype(jnp.int32) == family, col_at < row_at)
+    rank = jnp.sum(jnp.where(earlier, 1.0, 0.0), axis=1, keepdims=True)
+    slot = family * CAP + rank.astype(jnp.int32)
+    slot_row = jnp.sum(jnp.where(eye, slot.astype(F32), 0.0), axis=0, keepdims=True).astype(jnp.int32)
+    return slot, slot_row
+
+
+def unplace_kernel(pool, count, family_ref, out_ref, small_ref, fluct_ref, stress_ref, tangent_ref):
+    points = family_ref.shape[1]
+    slot, _ = slots_of(family_ref[...], pool)
+    taking = (slot == lax.broadcasted_iota(jnp.int32, (points, pool * CAP), 1)).astype(BF)
+    fluct_ref[...] = jnp.dot(taking, out_ref[...], preferred_element_type=F32).astype(BF)
+
+    @pl.when(pl.program_id(0) == 0)
+    def _():
+        small = sum(jnp.dot(taking, part, preferred_element_type=F32) for part in parts3(small_ref[...]))
+        tangent_ref[...] = small[:, 0:count * count]
+        at = lax.broadcasted_iota(jnp.int32, (PACK, LANES), 0) + count * count
+        picking = (at == lax.broadcasted_iota(jnp.int32, (PACK, LANES), 1)).astype(BF)
+        turned = sum(lax.dot_general(picking, part, NT, preferred_element_type=F32) for part in parts3(small))
+        stress_ref[...] = turned[0:count, :]
+
+
 def kernel(sizes, panel_ref, loads_ref, family_ref, contact_ref, strain_ref, previous_ref,
-           fluct_ref, stress_ref, tangent_ref,
-           held, whole, load, slot_prev, slot_contact, slot_strain, slot_out, slot_small,
+           slot_out, slot_small,
+           held, whole, load, slot_prev, slot_contact, slot_strain,
            iterate, residual, direction, inverse_ref, send_sem, recv_sem):
     macro, pool, plan, cut = sizes
     unit, most, lists, mirrored = plan
-    count, dof = loads_ref.shape[1], loads_ref.shape[2]
+    count, dof = loads_ref.shape[0], loads_ref.shape[2]
     rows = panel_ref.shape[1]
-    points = family_ref.shape[0]
+    points = family_ref.shape[1]
     slots = pool * CAP
     blocks = dof // LANES
     nz, nx = split_pool(pool)
@@ -108,7 +148,7 @@
                 held[m, my_pool, t * unit:(t + 1) * unit, :] = panel_ref[
                     0, low:low + unit, c * LANES:(c + 1) * LANES]
             for t, b in enumerate(range(m, blocks, macro)):
-                part = loads_ref[0, :, b * LANES:(b + 1) * LANES]
+                part = loads_ref[:, 0, b * LANES:(b + 1) * LANES]
                 part = jnp.concatenate([part, jnp.zeros((PACK - count, LANES), F32)], axis=0)
                 low = most * unit + t * PACK
                 held[m, my_pool, low:low + PACK, :] = part.astype(BF)
@@ -165,21 +205,20 @@
             along(src, h, path[i], ks[path[i]], at[path[i]])
         start(src, h, here, 1 - pc, None)
 
-    def event_z(kz):
-        for h in (0, 1):
-            event((kz, 0, 0), h)
-
-    def event_xy(kz):
-        for k in range(1, nx):
-            event((kz, k, 0), 0)
-        for k in range(1, ny):
-            event((kz, 0, k), 1)
-        for kx in range(nx):
-            for ky in range(1, ny):
-                event((kz, kx, ky), 0)
-        for ky in range(ny):
-            for kx in range(1, nx):
-                event((kz, kx, ky), 1)
+    def events_z(kz):
+        return [functools.partial(event, (kz, 0, 0), h) for h in (0, 1)] if kz < nz else []
+
+    def events_xy(kz):
+        if kz >= nz:
+            return []
+        first = [((kz, k, 0), 0) for k in range(1, nx)] + [((kz, 0, k), 1) for k in range(1, ny)]
+        second = [((kz, kx, ky), 0) for kx in range(nx) for ky in range(1, ny)]
+        second += [((kz, kx, ky), 1) for ky in range(ny) for kx in range(1, nx)]
+        return [functools.partial(event, ks, h) for ks, h in dict.fromkeys(first + second)]
+
+    def run(steps):
+        for step in steps:
+            step()
 
     def sibling(kz):
         for kx in range(nx):
@@ -188,33 +227,19 @@
                 for h in (0, 1):
                     arrive(device(at, 1 - pc), h)
 
-    event_z(0)
-
-    family = family_ref[...]
-    named = family == lax.broadcasted_iota(jnp.int32, (points, pool), 1)
-    row_at = lax.broadcasted_iota(jnp.int32, (points, points), 0)
-    col_at = lax.broadcasted_iota(jnp.int32, (points, points), 1)
-    before = jnp.dot((col_at < row_at).astype(BF), named.astype(BF), preferred_element_type=F32)
-    rank = jnp.sum(jnp.where(named, before, 0.0), axis=1, keepdims=True)
-    slot = family * CAP + rank.astype(jnp.int32)
-    slot_row = jnp.sum(jnp.where(row_at == col_at, slot.astype(F32), 0.0), axis=0, keepdims=True).astype(jnp.int32)
+    run(events_z(0))
+
+    _, slot_row = slots_of(family_ref[...], pool)
     placing = (lax.broadcasted_iota(jnp.int32, (slots, points), 0) == slot_row).astype(BF)
-    taking = (slot == lax.broadcasted_iota(jnp.int32, (points, slots), 1)).astype(BF)
-
-    def parts3(value):
-        high = value.astype(BF)
-        rest = value - high.astype(F32)
-        middle = rest.astype(BF)
-        return high, middle, (rest - middle.astype(F32)).astype(BF)
-
-    def move3(matrix, value):
-        return sum(jnp.dot(matrix, part, preferred_element_type=F32) for part in parts3(value))
 
     for i in range(count):
         span = slice(i * dof, (i + 1) * dof)
         slot_prev[:, span] = jnp.dot(placing, previous_ref[:, span], preferred_element_type=F32).astype(BF)
-    slot_contact[...] = move3(placing, contact_ref[...])
-    slot_strain[...] = move3(placing, strain_ref[...])
+    slot_contact[...] = sum(
+        jnp.dot(placing, part, preferred_element_type=F32) for part in parts3(contact_ref[...]))
+    slot_strain[...] = sum(
+        lax.dot_general(placing, part, NT, preferred_element_type=F32) for part in parts3(strain_ref[...]))
+    slot_small[...] = jnp.zeros_like(slot_small)
 
     eye = (lax.broadcasted_iota(jnp.int32, (LANES, LANES), 0)
            == lax.broadcasted_iota(jnp.int32, (LANES, LANES), 1))
@@ -235,7 +260,7 @@
             diagonal = jnp.sum(jnp.where(eye, whole[j, span, span].astype(F32), 0.0), axis=0, keepdims=True)
             inverse_ref[j, :, span] = 1.0 / diagonal
 
-    def solve_pair(pair):
+    def solve_pair(pair, between):
         at16 = pl.ds(pl.multiple_of(pair * 2 * CAP, 2 * CAP), 2 * CAP)
         for j in (0, 1):
             assemble(j, pair * 2 + j)
@@ -262,7 +287,7 @@
             direction[j] = scaled
             current.append(jnp.sum(left * scaled, axis=-1, keepdims=True))
 
-        def sweep(_, current):
+        def sweep(current):
             after = []
             for j in (0, 1):
                 toward = direction[j]
@@ -275,9 +300,12 @@
                 residual[j] = left
                 direction[j] = scaled + (updated / (current[j] + 1e-6)) * toward
                 after.append(updated)
-            return tuple(after)
-
-        lax.fori_loop(0, ITERS, sweep, tuple(current))
+            return after
+
+        between()
+        for _ in range(ITERS):
+            current = sweep(current)
+            between()
 
         for i in range(count):
             span = slice(i * CAP, (i + 1) * CAP)
@@ -289,9 +317,8 @@
             high = value.astype(BF)
             low = (value - high.astype(F32)).astype(BF)
             weights = load[j]
-            contract = (((1,), (1,)), ((), ()))
-            tang = (lax.dot_general(high, weights, contract, preferred_element_type=F32)
-                    + lax.dot_general(low, weights, contract, preferred_element_type=F32)) * (1.0 / dof)
+            tang = (lax.dot_general(high, weights, NT, preferred_element_type=F32)
+                    + lax.dot_general(low, weights, NT, preferred_element_type=F32)) * (1.0 / dof)
             strain = slot_strain[mine, :]
             for i in range(count):
                 piece = tang[i * CAP:(i + 1) * CAP, 0:count]
@@ -299,24 +326,21 @@
                 slot_small[mine, count * count + i:count * count + i + 1] = jnp.sum(
                     piece * strain, axis=-1, keepdims=True)
 
-    def solve(kz):
+    def solve(kz, steps):
         at = pick(orders[0], pz, kz) if kz else pz
+        share = -(-len(steps) // (ITERS + 1))
+
+        def between():
+            run(steps[:share])
+            del steps[:share]
+
         for q in range(nx // 2):
-            solve_pair(at * (nx // 2) + q)
-
+            solve_pair(at * (nx // 2) + q, between)
+
+    run(events_z(1) + events_xy(0) + events_z(2))
     for kz in range(nz):
-        if kz + 1 < nz:
-            event_z(kz + 1)
-        event_xy(kz)
         sibling(kz)
-        solve(kz)
-
-    for i in range(count):
-        span = slice(i * dof, (i + 1) * dof)
-        fluct_ref[:, span] = jnp.dot(taking, slot_out[:, span], preferred_element_type=F32).astype(BF)
-    small = move3(taking, slot_small[...])
-    tangent_ref[...] = small[:, 0:count * count]
-    stress_ref[...] = small[:, count * count:count * count + count]
+        solve(kz, events_z(kz + 3) + events_xy(kz + 1))
 
     for copy, cond in pending:
         if cond is None:
@@ -350,15 +374,15 @@
     slots = pool * CAP
     nz, nx = split_pool(pool)
     vmem = pl.BlockSpec(memory_space=pltpu.VMEM)
-    return pl.pallas_call(
+    family_row = family.T
+    slot_out, slot_small = pl.pallas_call(
         functools.partial(kernel, (macro, pool, plan, cut)),
         out_shape=(
-            jax.ShapeDtypeStruct(previous.shape, BF),
-            jax.ShapeDtypeStruct((points, count), F32),
-            jax.ShapeDtypeStruct((points, count * count), F32),
+            jax.ShapeDtypeStruct((slots, count * dof), BF),
+            jax.ShapeDtypeStruct((slots, LANES), F32),
         ),
         in_specs=[vmem] * 6,
-        out_specs=(vmem,) * 3,
+        out_specs=(vmem,) * 2,
         scratch_shapes=[
             pltpu.VMEM((macro, pool, total_rows, LANES), BF),
             pltpu.VMEM((2, dof, dof), BF),
@@ -366,8 +390,6 @@
             pltpu.VMEM((slots, count * dof), BF),
             pltpu.VMEM((slots, dof), F32),
             pltpu.VMEM((slots, count), F32),
-            pltpu.VMEM((slots, count * dof), BF),
-            pltpu.VMEM((slots, LANES), F32),
             pltpu.VMEM((2, count * CAP, dof), F32),
             pltpu.VMEM((2, count * CAP, dof), F32),
             pltpu.VMEM((2, count * CAP, dof), F32),
@@ -377,7 +399,27 @@
         ],
         compiler_params=pltpu.CompilerParams(
             collective_id=0, has_side_effects=True, vmem_limit_bytes=56 * 1024 * 1024),
-    )(panels, loads, family, contact, strain, previous)
+    )(panels, loads.transpose(1, 0, 2), family_row, contact, strain.T, previous)
+    fluct, stress, tangent = pl.pallas_call(
+        functools.partial(unplace_kernel, pool, count),
+        grid=(count,),
+        out_shape=(
+            jax.ShapeDtypeStruct(previous.shape, BF),
+            jax.ShapeDtypeStruct((count, points), F32),
+            jax.ShapeDtypeStruct((points, count * count), F32),
+        ),
+        in_specs=[
+            pl.BlockSpec((1, points), lambda i: (0, 0)),
+            pl.BlockSpec((slots, dof), lambda i: (0, i)),
+            pl.BlockSpec((slots, LANES), lambda i: (0, 0)),
+        ],
+        out_specs=(
+            pl.BlockSpec((points, dof), lambda i: (0, i)),
+            pl.BlockSpec((count, points), lambda i: (0, 0)),
+            pl.BlockSpec((points, count * count), lambda i: (0, 0)),
+        ),
+    )(family_row, slot_out, slot_small)
+    return fluct, stress.T, tangent
 
 
 def solution(mesh):

time: 74.7 us -> 62.8 us (0.84)
  local copies, waits for them, and re-layouts: 6.93 us -> 0 us
  Pallas kernels: 66.7 us -> 61.8 us
    pallas_call x1, Pallas kernels: 66.7 us -> 54.5 us  [on_device(): pl.pallas_call(functools.partial(kernel, (macro, pool, plan, cut)), out_s...]
    pallas_call x0 -> x1, Pallas kernels: none -> 7.23 us  [on_device(): pl.pallas_call(functools.partial(unplace_kernel, pool, count), grid=(coun...]
    unnamed x11 -> x0, local copies, waits for them, and re-layouts: 5.5 us -> none
    pallas_call x1 -> x0, local copies, waits for them, and re-layouts: 1.43 us -> none  [on_device(): pl.pallas_call(functools.partial(kernel, (macro, pool, plan, cut)), out_s...]
where the time goes in v2:
time: 62.8 us; the launch traced here: 62.4 us
  Pallas kernels  61.8 us (98%)
  between operations  0.64 us (1%)
    pallas_call x1, Pallas kernels, on_device(): pl.pallas_call(functools.partial(kernel, (macro, pool, plan, cut)), out_s...  54.5 us
    pallas_call x1, Pallas kernels, on_device(): pl.pallas_call(functools.partial(unplace_kernel, pool, count), grid=(coun...  7.23 us

profile of v2, /device:TPU:0, one launch (start us, length us, event | category | flops | bytes accessed | tf_op | source)
XLA Modules:
  0.0 62.4 jit_solution(13543789180843061521)
XLA Ops:
  0.6 54.5 %shard_map.85 = (bf16[64,6912]{1,0:T(8,128)(2,1)}, f32[64,128]{1,0:T(8,128)}) custom-call(bf16[1,192,768]{2,1,0:T(8,128)(2,1)} %panel_ref.1, f32[9,1,768]{2,1,0:T(1,128)} %bitcast.4, s32[1,64]{1,0:T(1,128)} %bitcast.6, f32[64,768]{1,0:T(8,128)} %contact_ref.1, f32[9,64]{1,0:T(8,128)} %bitcast.5, bf16[64,6912]{1,0:T(8,128)(2,1)} %previous_ref.1), custom_call_target="tpu_custom_call" | custom-call | tf_op jit(solution)/shard_map/pallas_call | solution.py:378
  55.2 7.2 %shard_map.86 = (bf16[64,6912]{1,0:T(8,128)(2,1)}, f32[9,64]{1,0:T(8,128)}, f32[64,81]{1,0:T(8,128)}) custom-call(s32[1,64]{1,0:T(1,128)} %bitcast.7, bf16[64,6912]{1,0:T(8,128)(2,1)} %get-tuple-element.8.out_ref, f32[64,128]{1,0:T(8,128)} %get-tuple-element.9.small_ref), custom_call_target="tpu_custom_call" | custom-call | tf_op jit(solution)/shard_map/pallas_call | solution.py:403

commit v3 on v2

--- a/solution.py
+++ b/solution.py
@@ -84,21 +84,18 @@
     slot, _ = slots_of(family_ref[...], pool)
     taking = (slot == lax.broadcasted_iota(jnp.int32, (points, pool * CAP), 1)).astype(BF)
     fluct_ref[...] = jnp.dot(taking, out_ref[...], preferred_element_type=F32).astype(BF)
-
-    @pl.when(pl.program_id(0) == 0)
-    def _():
-        small = sum(jnp.dot(taking, part, preferred_element_type=F32) for part in parts3(small_ref[...]))
-        tangent_ref[...] = small[:, 0:count * count]
-        at = lax.broadcasted_iota(jnp.int32, (PACK, LANES), 0) + count * count
-        picking = (at == lax.broadcasted_iota(jnp.int32, (PACK, LANES), 1)).astype(BF)
-        turned = sum(lax.dot_general(picking, part, NT, preferred_element_type=F32) for part in parts3(small))
-        stress_ref[...] = turned[0:count, :]
+    small = sum(jnp.dot(taking, part, preferred_element_type=F32) for part in parts3(small_ref[...]))
+    tangent_ref[...] = small[:, 0:count * count]
+    at = lax.broadcasted_iota(jnp.int32, (PACK, LANES), 0) + count * count
+    picking = (at == lax.broadcasted_iota(jnp.int32, (PACK, LANES), 1)).astype(BF)
+    turned = sum(lax.dot_general(picking, part, NT, preferred_element_type=F32) for part in parts3(small))
+    stress_ref[...] = turned[0:count, :]
 
 
 def kernel(sizes, panel_ref, loads_ref, family_ref, contact_ref, strain_ref, previous_ref,
            slot_out, slot_small,
            held, whole, load, slot_prev, slot_contact, slot_strain,
-           iterate, residual, direction, inverse_ref, send_sem, recv_sem):
+           iterate, residual, direction, product, inverse_ref, send_sem, recv_sem):
     macro, pool, plan, cut = sizes
     unit, most, lists, mirrored = plan
     count, dof = loads_ref.shape[0], loads_ref.shape[2]
@@ -258,7 +255,7 @@
         for r in range(blocks):
             span = slice(r * LANES, (r + 1) * LANES)
             diagonal = jnp.sum(jnp.where(eye, whole[j, span, span].astype(F32), 0.0), axis=0, keepdims=True)
-            inverse_ref[j, :, span] = 1.0 / diagonal
+            inverse_ref[j, :, span] = jnp.broadcast_to(1.0 / diagonal, (CAP, LANES))
 
     def solve_pair(pair, between):
         at16 = pl.ds(pl.multiple_of(pair * 2 * CAP, 2 * CAP), 2 * CAP)
@@ -272,34 +269,40 @@
         def contact_of(j):
             return slot_contact[pl.ds(pl.multiple_of(pair * 2 * CAP + j * CAP, CAP), CAP), :]
 
-        def apply(j, field):
-            product = jnp.dot(field.astype(BF), whole[j], preferred_element_type=F32)
-            extra = contact_of(j)[None, :, :] * field.reshape(count, CAP, dof)
-            return product + extra.reshape(count * CAP, dof)
-
+        cases = [slice(i * CAP, (i + 1) * CAP) for i in range(count)]
+
+        def multiply(field):
+            for j in (0, 1):
+                product[j] = jnp.dot(field[j].astype(BF), whole[j], preferred_element_type=F32)
+
+        multiply(iterate)
         current = []
         for j in (0, 1):
-            loads = load[j, 0:count, :].astype(F32)
-            wide = jnp.broadcast_to(loads[:, None, :], (count, CAP, dof)).reshape(count * CAP, dof)
-            left = wide - apply(j, iterate[j])
-            scaled = inverse_ref[j] * left
-            residual[j] = left
-            direction[j] = scaled
-            current.append(jnp.sum(left * scaled, axis=-1, keepdims=True))
+            extra, inverse = contact_of(j), inverse_ref[j]
+            for i, case in enumerate(cases):
+                left = load[j, i:i + 1, :].astype(F32) - (product[j, case, :] + extra * iterate[j, case, :])
+                scaled = inverse * left
+                residual[j, case, :] = left
+                direction[j, case, :] = scaled
+                current.append(jnp.sum(left * scaled, axis=-1, keepdims=True))
 
         def sweep(current):
+            multiply(direction)
             after = []
             for j in (0, 1):
-                toward = direction[j]
-                image = apply(j, toward)
-                step = current[j] / (jnp.sum(toward * image, axis=-1, keepdims=True) + 1e-6)
-                iterate[j] = iterate[j] + step * toward
-                left = residual[j] - step * image
-                scaled = inverse_ref[j] * left
-                updated = jnp.sum(left * scaled, axis=-1, keepdims=True)
-                residual[j] = left
-                direction[j] = scaled + (updated / (current[j] + 1e-6)) * toward
-                after.append(updated)
+                extra, inverse = contact_of(j), inverse_ref[j]
+                for i, case in enumerate(cases):
+                    before = current[j * count + i]
+                    toward = direction[j, case, :]
+                    image = product[j, case, :] + extra * toward
+                    step = before / (jnp.sum(toward * image, axis=-1, keepdims=True) + 1e-6)
+                    iterate[j, case, :] = iterate[j, case, :] + step * toward
+                    left = residual[j, case, :] - step * image
+                    scaled = inverse * left
+                    updated = jnp.sum(left * scaled, axis=-1, keepdims=True)
+                    residual[j, case, :] = left
+                    direction[j, case, :] = scaled + (updated / (before + 1e-6)) * toward
+                    after.append(updated)
             return after
 
         between()
@@ -393,7 +396,8 @@
             pltpu.VMEM((2, count * CAP, dof), F32),
             pltpu.VMEM((2, count * CAP, dof), F32),
             pltpu.VMEM((2, count * CAP, dof), F32),
-            pltpu.VMEM((2, 1, dof), F32),
+            pltpu.VMEM((2, count * CAP, dof), F32),
+            pltpu.VMEM((2, CAP, dof), F32),
             pltpu.SemaphoreType.DMA((count_sends(nz, nx, macro // CORES),)),
             pltpu.SemaphoreType.DMA((macro, pool, 2)),
         ],
@@ -402,22 +406,14 @@
     )(panels, loads.transpose(1, 0, 2), family_row, contact, strain.T, previous)
     fluct, stress, tangent = pl.pallas_call(
         functools.partial(unplace_kernel, pool, count),
-        grid=(count,),
         out_shape=(
             jax.ShapeDtypeStruct(previous.shape, BF),
             jax.ShapeDtypeStruct((count, points), F32),
             jax.ShapeDtypeStruct((points, count * count), F32),
         ),
-        in_specs=[
-            pl.BlockSpec((1, points), lambda i: (0, 0)),
-            pl.BlockSpec((slots, dof), lambda i: (0, i)),
-            pl.BlockSpec((slots, LANES), lambda i: (0, 0)),
-        ],
-        out_specs=(
-            pl.BlockSpec((points, dof), lambda i: (0, i)),
-            pl.BlockSpec((count, points), lambda i: (0, 0)),
-            pl.BlockSpec((points, count * count), lambda i: (0, 0)),
-        ),
+        in_specs=[vmem] * 3,
+        out_specs=(vmem,) * 3,
+        compiler_params=pltpu.CompilerParams(vmem_limit_bytes=32 * 1024 * 1024),
     )(family_row, slot_out, slot_small)
     return fluct, stress.T, tangent
 

time: 62.8 us -> 59.4 us (0.946)
  Pallas kernels: 61.8 us -> 55.9 us
  local copies, waits for them, and re-layouts: 0 us -> 2.57 us
    pallas_call x1, Pallas kernels: 7.23 us -> 1.45 us  [on_device(): pl.pallas_call(functools.partial(unplace_kernel, pool, count), out_shape=...]
    unnamed x0 -> x6, local copies, waits for them, and re-layouts: none -> 2.57 us
where the time goes in v3:
time: 59.4 us; the launch traced here: 59.2 us
  Pallas kernels  55.9 us (94%)
  local copies, waits for them, and re-layouts  2.57 us (4%)
  between operations  0.65 us (1%)
    pallas_call x1, Pallas kernels, on_device(): pl.pallas_call(functools.partial(kernel, (macro, pool, plan, cut)), out_s...  54.5 us
    unnamed x6, local copies, waits for them, and re-layouts  2.57 us
    pallas_call x1, Pallas kernels, on_device(): pl.pallas_call(functools.partial(unplace_kernel, pool, count), out_shape=...  1.45 us

profile of v3, /device:TPU:0, one launch (start us, length us, event | category | flops | bytes accessed | tf_op | source)
XLA Modules:
  0.0 59.2 jit_solution(4025626789466603937)
XLA Ops:
  0.6 54.5 %shard_map.85 = (bf16[64,6912]{1,0:T(8,128)(2,1)}, f32[64,128]{1,0:T(8,128)}) custom-call(bf16[1,192,768]{2,1,0:T(8,128)(2,1)} %panel_ref.1, f32[9,1,768]{2,1,0:T(1,128)} %bitcast.6, s32[1,64]{1,0:T(1,128)} %bitcast.4, f32[64,768]{1,0:T(8,128)} %contact_ref.1, f32[9,64]{1,0:T(8,128)} %bitcast.7, bf16[64,6912]{1,0:T(8,128)(2,1)} %previous_ref.1), custom_call_target="tpu_custom_call" | custom-call | tf_op jit(solution)/shard_map/pallas_call | solution.py:381
  55.1 0.0 copy-start.2
  55.1 0.6 %copy-done.2 = s32[64,1]{0,1:T(1,128)S(1)} copy-done((s32[64,1]{0,1:T(1,128)S(1)}, s32[64,1]{0,1:T(1,128)}, u32[]{:S(2)}) %copy-start.2) | copy-done | bytes 280
  55.8 0.0 copy-start
  55.8 1.2 %copy-done = bf16[64,6912]{1,0:T(8,128)(2,1)S(1)} copy-done((bf16[64,6912]{1,0:T(8,128)(2,1)S(1)}, bf16[64,6912]{1,0:T(8,128)(2,1)}, u32[]{:S(2)}) %copy-start) | copy-done | bytes 884760
  57.0 0.0 copy-start.1
  57.0 0.8 %copy-done.1 = f32[64,128]{1,0:T(8,128)S(1)} copy-done((f32[64,128]{1,0:T(8,128)S(1)}, f32[64,128]{1,0:T(8,128)}, u32[]{:S(2)}) %copy-start.1) | copy-done | bytes 32792
  57.7 1.4 %shard_map.86 = (bf16[64,6912]{1,0:T(8,128)(2,1)}, f32[9,64]{1,0:T(8,128)}, f32[64,81]{1,0:T(8,128)}) custom-call(s32[1,64]{1,0:T(1,128)S(1)} %bitcast.5, bf16[64,6912]{1,0:T(8,128)(2,1)S(1)} %copy-done, f32[64,128]{1,0:T(8,128)S(1)} %copy-done.1), custom_call_target="tpu_custom_call" | custom-call | tf_op jit(solution)/shard_map/pallas_call | solution.py:407
Async XLA Ops:
  55.1 0.7 %copy-start.2 = (s32[64,1]{0,1:T(1,128)S(1)}, s32[64,1]{0,1:T(1,128)}, u32[]{:S(2)}) copy-start(s32[64,1]{0,1:T(1,128)} %param.8) | copy-start | bytes 772
  55.8 1.2 %copy-start = (bf16[64,6912]{1,0:T(8,128)(2,1)S(1)}, bf16[64,6912]{1,0:T(8,128)(2,1)}, u32[]{:S(2)}) copy-start(bf16[64,6912]{1,0:T(8,128)(2,1)} %get-tuple-element.8.out_ref) | copy-start | bytes 2654212
  57.0 0.8 %copy-start.1 = (f32[64,128]{1,0:T(8,128)S(1)}, f32[64,128]{1,0:T(8,128)}, u32[]{:S(2)}) copy-start(f32[64,128]{1,0:T(8,128)} %get-tuple-element.9.small_ref) | copy-start | bytes 98308

commit v4 on v3

--- a/solution.py
+++ b/solution.py
@@ -55,6 +55,7 @@
     return out
 
 
+PATHS = ((0, 1, 2), (0, 2, 1), (1, 2, 0))
 NT = (((1,), (1,)), ((), ()))
 
 
@@ -106,7 +107,7 @@
     nz, nx = split_pool(pool)
     ny = macro // CORES
     total_rows = held.shape[2]
-    cuts = ((0, cut), (cut, total_rows - cut))
+    cuts = ((0, cut[0]), (cut[0], cut[1] - cut[0]), (cut[1], total_rows - cut[1]))
 
     my_macro, my_pool = lax.axis_index("macro"), lax.axis_index("pool")
     pz, px = my_pool // nx, my_pool % nx
@@ -186,7 +187,6 @@
             to = jnp.where(p > source, p + 1, p - 1)
             start(src, h, moved(axis, to), pc, jnp.logical_and(to >= 0, to < n))
 
-    paths = ((0, 1, 2), (0, 2, 1))
 
     def sources(ks):
         return tuple(here[a] if ks[a] == 0 else pick(orders[a], here[a], ks[a]) for a in range(3))
@@ -196,7 +196,7 @@
         src = device(at, pc)
         if any(ks):
             arrive(src, h)
-        path = paths[h]
+        path = PATHS[h]
         last = max([i for i in range(3) if ks[path[i]]], default=0)
         for i in range(last, 3):
             along(src, h, path[i], ks[path[i]], at[path[i]])
@@ -213,6 +213,13 @@
         second += [((kz, kx, ky), 1) for ky in range(ny) for kx in range(1, nx)]
         return [functools.partial(event, ks, h) for ks, h in dict.fromkeys(first + second)]
 
+    def events_last(kz):
+        if kz >= nz:
+            return []
+        first = [(kz, k, 0) for k in range(0 if kz else 1, nx)]
+        second = [(kz, kx, ky) for kx in range(nx) for ky in range(1, ny)]
+        return [functools.partial(event, ks, 2) for ks in first + second]
+
     def run(steps):
         for step in steps:
             step()
@@ -221,10 +228,11 @@
         for kx in range(nx):
             for ky in range(ny):
                 at = sources((kz, kx, ky))
-                for h in (0, 1):
+                for h in range(len(PATHS)):
                     arrive(device(at, 1 - pc), h)
 
     run(events_z(0))
+    event((0, 0, 0), 2)
 
     _, slot_row = slots_of(family_ref[...], pool)
     placing = (lax.broadcasted_iota(jnp.int32, (slots, points), 0) == slot_row).astype(BF)
@@ -340,10 +348,10 @@
         for q in range(nx // 2):
             solve_pair(at * (nx // 2) + q, between)
 
-    run(events_z(1) + events_xy(0) + events_z(2))
+    run(events_z(1) + events_xy(0) + events_last(0) + events_z(2) + events_last(1))
     for kz in range(nz):
         sibling(kz)
-        solve(kz, events_z(kz + 3) + events_xy(kz + 1))
+        solve(kz, events_z(kz + 3) + events_xy(kz + 1) + events_last(kz + 2))
 
     for copy, cond in pending:
         if cond is None:
@@ -359,7 +367,7 @@
         return 1 if n == 2 or k > 0 else 2
 
     total = 0
-    for path in ((0, 1, 2), (0, 2, 1)):
+    for path in PATHS:
         for ks in itertools.product(range(nz), range(nx), range(ny)):
             last = max([i for i in range(3) if ks[path[i]]], default=0)
             total += 1 + sum(along((nz, nx, ny)[path[i]], ks[path[i]]) for i in range(last, 3))
@@ -373,7 +381,9 @@
     unit, most = plan[0], plan[1]
     shares = -(-(dof // LANES) // macro)
     total_rows = most * unit + shares * PACK
-    cut = -(-total_rows // (2 * PACK)) * PACK
+    last = (2 * total_rows // 9 + PACK // 2) // PACK * PACK
+    first = -(-(total_rows - last) // (2 * PACK)) * PACK
+    cut = (first, total_rows - last)
     slots = pool * CAP
     nz, nx = split_pool(pool)
     vmem = pl.BlockSpec(memory_space=pltpu.VMEM)
@@ -399,7 +409,7 @@
             pltpu.VMEM((2, count * CAP, dof), F32),
             pltpu.VMEM((2, CAP, dof), F32),
             pltpu.SemaphoreType.DMA((count_sends(nz, nx, macro // CORES),)),
-            pltpu.SemaphoreType.DMA((macro, pool, 2)),
+            pltpu.SemaphoreType.DMA((macro, pool, len(PATHS))),
         ],
         compiler_params=pltpu.CompilerParams(
             collective_id=0, has_side_effects=True, vmem_limit_bytes=56 * 1024 * 1024),
@@ -413,7 +423,7 @@
         ),
         in_specs=[vmem] * 3,
         out_specs=(vmem,) * 3,
-        compiler_params=pltpu.CompilerParams(vmem_limit_bytes=32 * 1024 * 1024),
+        compiler_params=pltpu.CompilerParams(vmem_limit_bytes=56 * 1024 * 1024),
     )(family_row, slot_out, slot_small)
     return fluct, stress.T, tangent
 

time: 59.4 us -> 58.9 us (level)
  local copies, waits for them, and re-layouts: 2.57 us -> 0 us
  Pallas kernels: 55.9 us -> 58.1 us
    unnamed x6 -> x0, local copies, waits for them, and re-layouts: 2.57 us -> none
    pallas_call x1, Pallas kernels: 1.45 us -> 2.63 us  [on_device(): pl.pallas_call(functools.partial(unplace_kernel, pool, count), out_shape=...]
    pallas_call x1, Pallas kernels: 54.5 us -> 55.5 us  [on_device(): pl.pallas_call(functools.partial(kernel, (macro, pool, plan, cut)), out_s...]
where the time goes in v4:
time: 58.9 us; the launch traced here: 58.8 us
  Pallas kernels  58.1 us (99%)
  between operations  0.64 us (1%)
    pallas_call x1, Pallas kernels, on_device(): pl.pallas_call(functools.partial(kernel, (macro, pool, plan, cut)), out_s...  55.5 us
    pallas_call x1, Pallas kernels, on_device(): pl.pallas_call(functools.partial(unplace_kernel, pool, count), out_shape=...  2.63 us

profile of v4, /device:TPU:0, one launch (start us, length us, event | category | flops | bytes accessed | tf_op | source)
XLA Modules:
  0.0 58.8 jit_solution(14080338520629167484)
XLA Ops:
  0.6 55.5 %shard_map.85 = (bf16[64,6912]{1,0:T(8,128)(2,1)}, f32[64,128]{1,0:T(8,128)}) custom-call(bf16[1,192,768]{2,1,0:T(8,128)(2,1)} %panel_ref.1, f32[9,1,768]{2,1,0:T(1,128)} %bitcast.4, s32[1,64]{1,0:T(1,128)} %bitcast.6, f32[64,768]{1,0:T(8,128)} %contact_ref.1, f32[9,64]{1,0:T(8,128)} %bitcast.5, bf16[64,6912]{1,0:T(8,128)(2,1)} %previous_ref.1), custom_call_target="tpu_custom_call" | custom-call | tf_op jit(solution)/shard_map/pallas_call | solution.py:391
  56.1 2.6 %shard_map.86 = (bf16[64,6912]{1,0:T(8,128)(2,1)}, f32[9,64]{1,0:T(8,128)}, f32[64,81]{1,0:T(8,128)}) custom-call(s32[1,64]{1,0:T(1,128)} %bitcast.7, bf16[64,6912]{1,0:T(8,128)(2,1)} %get-tuple-element.8.out_ref, f32[64,128]{1,0:T(8,128)} %get-tuple-element.9.small_ref), custom_call_target="tpu_custom_call" | custom-call | tf_op jit(solution)/shard_map/pallas_call | solution.py:417
